TPU v7x, 256 devices: a whole 4x4x8 slice. The times are simulated.
256 devices in a mesh: ja: 16 (over y_hi, x, core), aa: 16 (over y_lo, z).
Axes of the slice: x: 4, y: 4 (y_hi: 2, y_lo: 2; y = y_hi * 2 + y_lo), z: 8, core: 2. Of those that a mesh axis runs over, the one named last changes fastest.
Arguments:
- amplitudes: float32 [2, 64, 1024, 1024], P(None, 'ja', 'aa'), may hold values from -6 to 6
- chol: float32 [2, 1024, 1024], P(None, 'ja'), as said below
- irrep_i: int32 [2], replicated, may hold values from 0 to 7
- irrep_j: int32 [64], replicated, may hold values from 0 to 7
- irrep_v: int32 [1024], replicated, may hold values from 0 to 7
- irrep_l: int32 [2], replicated, may hold values from 0 to 7
Outputs:
- ladder: float32 [2, 64, 1024, 1024], P(None, 'ja', 'aa')
Inputs may be any that keep to these rules, and one draw needn't show every extreme that they name: chol[l] is symmetric in its last two indices.
All inputs are finite; a program needn't handle non-finite values.
Results may differ from a plain program's by a relative error of at most 0.0003.
Values sent between devices are 32-bit elements; how exact they have to be, the bound alone decides.
No kernel may reach another device: no remote copies, remote signals or barrier semaphores. Data moves between devices by JAX's collectives and lax.ppermute only.
A program may use at most 128 MiB of HBM per device.

v0:
```python
import jax
import jax.numpy as jnp
from jax import lax
from jax.experimental import pallas as pl
from jax.experimental.pallas import tpu as pltpu
from jax.sharding import PartitionSpec as P

F32, BF16, I32 = jnp.float32, jnp.bfloat16, jnp.int32
NN = (((1,), (0,)), ((), ()))
NT = (((1,), (1,)), ((), ()))
SLOTS = 32
RANKS = 16
CLS, NUM, SLOT, SPOT, LAB, RANK, FLAG, BITS = range(8)


def iota(shape, dim):
    return lax.broadcasted_iota(I32, shape, dim)


def parity(x):
    return (x ^ (x >> 1) ^ (x >> 2)) & 1


def one(cond):
    return jnp.where(cond, 1.0, 0.0).astype(F32)


def dot(a, b, dims=NN):
    return lax.dot_general(a, b, dims, preferred_element_type=F32)


def split(x):
    high = x.astype(BF16)
    return high, (x - high.astype(F32)).astype(BF16)


def dot3(a, b, dims=NN):
    (ah, al), (bh, bl) = a, b
    return dot(ah, bh, dims) + dot(ah, bl, dims) + dot(al, bh, dims)


def dot2(a, b, dims=NN):
    return dot(a, b[0], dims) + dot(a, b[1], dims)


def table_kernel(irrep_ref, l_ref, row_ref, col_ref):
    cls = irrep_ref[...]
    width = cls.shape[1]
    chunks = width // 128
    onehot = one(cls == iota((16, width), 0))
    before = one(iota((128, 128), 0) < iota((128, 128), 1))
    count = jnp.zeros((16, 1), F32)
    blocks = jnp.zeros((16, 128), F32)
    slots = []
    for k in range(chunks):
        part = onehot[:, 128 * k : 128 * k + 128]
        ahead = dot(part.astype(BF16), before.astype(BF16)) + count
        slots.append(jnp.sum(part * ahead, axis=0, keepdims=True))
        count = count + jnp.sum(part, axis=1, keepdims=True)
        place = one(iota((128, 128), 1) == 2 * k + (iota((128, 128), 0) >> 6))
        blocks = blocks + dot(part.astype(BF16), place.astype(BF16))
    slot = jnp.concatenate(slots, axis=1).astype(I32)
    lane = iota((16, 128), 1)
    cand = iota((16, 128), 0)
    count_lane = jnp.sum(jnp.where(lane == cand, count, 0.0), axis=0, keepdims=True)
    member = (parity((cand >> 1) & lane) == (cand & 1)) & (lane < 8)
    largest = jnp.max(jnp.where(member, count_lane, 0.0), axis=1, keepdims=True)
    in_block = jnp.zeros((16, 128), F32)
    for g in range(8):
        in_block = in_block + jnp.where(parity((cand >> 1) & g) == (cand & 1), blocks[g : g + 1, :], 0.0)
    fullest = jnp.max(in_block, axis=1, keepdims=True)
    bits_col = cand[:, 0:1] >> 1
    good = (largest <= SLOTS) & (fullest <= RANKS)
    for n in range(l_ref.shape[0]):
        good = good & (parity(bits_col & l_ref[n]) == 1)
    pick = jnp.min(jnp.where(good, cand[:, 0:1].astype(F32), 99.0), axis=0, keepdims=True).astype(I32)
    bits, side = pick >> 1, pick & 1
    small = parity(bits & cls) == side
    group = jnp.zeros_like(cls)
    label = jnp.zeros_like(cls)
    lane_group = iota((1, width), 1) >> 5
    number = jnp.zeros((1, 1), I32)
    for g in range(8):
        is_small = parity(bits & g) == side
        group = group + jnp.where(is_small & (cls > g), 1, 0)
        label = label + jnp.where(is_small & (number == lane_group), g, 0)
        number = number + jnp.where(is_small, 1, 0)
    inner = one((iota((128, 128), 0) < iota((128, 128), 1)) & ((iota((128, 128), 0) >> 6) == (iota((128, 128), 1) >> 6)))
    small16 = jnp.broadcast_to(one(small), (16, width))
    ranks = [
        dot(small16[:, 128 * k : 128 * k + 128].astype(BF16), inner.astype(BF16))[0:1, :] for k in range(chunks)
    ]
    rank = jnp.concatenate(ranks, axis=1).astype(I32)
    none = jnp.full_like(cls, -1)
    table = jnp.concatenate(
        [
            cls,
            jnp.where(small, group * SLOTS + slot, none),
            jnp.where(small, slot, none),
            jnp.where(small, (iota((1, width), 1) >> 6) * RANKS + rank, none),
            label,
            jnp.where(small, rank, none),
            jnp.broadcast_to(jnp.where(pick < 99, 1, 0), cls.shape),
            jnp.broadcast_to(bits, cls.shape),
        ],
        axis=0,
    )
    row_ref[...] = table
    table = table.astype(F32)
    for k in range(chunks):
        tile = jnp.concatenate([table[:, 128 * k : 128 * k + 128], jnp.zeros((120, 128), F32)], axis=0)
        col_ref[128 * k : 128 * k + 128, :] = jnp.transpose(tile).astype(I32)


def own(col_ref, block, field):
    return col_ref[pl.ds(pl.multiple_of(block * 64, 64), 64), field : field + 1]


def panel_kernel(row_ref, col_ref, chol_ref, l_ref, pos_ref, out_ref):
    cls = row_ref[CLS : CLS + 1, :]
    slot = row_ref[SLOT : SLOT + 1, :]
    own_cls = own(col_ref, pos_ref[0], CLS)
    pick = one(slot == iota((SLOTS, slot.shape[1]), 0)).astype(BF16)
    parts = []
    for n in range(2):
        kept = jnp.where((own_cls ^ cls) == l_ref[n], chol_ref[n], 0.0)
        high, low = split(kept)
        parts.append(dot(high, pick, NT) + dot(low, pick, NT))
    both = jnp.concatenate(parts, axis=1)
    packed = jnp.concatenate([both[0:32], both[32:64]], axis=1)
    out_ref[...] = jnp.broadcast_to(packed[None], out_ref.shape)


def unpack(gathered):
    n = gathered.shape[0]
    return jnp.concatenate([gathered, jnp.roll(gathered, 64, axis=2)], axis=1).reshape(n * 64, 128)


def places(row_ref):
    spot = row_ref[SPOT : SPOT + 1, :]
    number = row_ref[NUM : NUM + 1, :]
    width = spot.shape[1]
    spots = one(spot == iota((16 * RANKS, width), 0)).astype(BF16)
    numbers = one(number == iota((4 * SLOTS, width), 0)).astype(BF16)
    return spots, numbers


def half_kernel(row_ref, col_ref, amp_ref, got_ref, i_ref, j_ref, l_ref, pos_ref, out_ref, high_ref, low_ref):
    p, q = pos_ref[0], pos_ref[1]
    cls = row_ref[CLS : CLS + 1, :]
    label = row_ref[LAB : LAB + 1, 0:128]
    own_cls = own(col_ref, q, CLS)
    own_small = own(col_ref, q, NUM) >= 0
    own_rank = own(col_ref, q, RANK)
    xs = [i_ref[n // 4] ^ j_ref[p * 4 + n % 4] for n in range(8)]
    for n in range(8):
        kept = jnp.where((own_cls ^ cls) == xs[n], amp_ref[n // 4, n % 4], 0.0)
        high_ref[64 * n : 64 * n + 64, :], low_ref[64 * n : 64 * n + 64, :] = split(kept)
    panel = unpack(got_ref[...])
    lane = iota(panel.shape, 1)
    slot = col_ref[:, SLOT : SLOT + 1]
    weights = jnp.where(lane < 64, panel, one(slot == lane - 64))
    wh, wl = split(weights)
    first = dot(high_ref[...], jnp.concatenate([wh, wl], axis=1))
    half = first[:, 0:128] + first[:, 128:256] + dot(low_ref[...], wh)
    parts = [half[64 * n : 64 * n + 64] for n in range(8)]
    firsts = [part[:, 64:96] + jnp.where(own_small, part[:, 0:32], 0.0) for part in parts]
    own_panel = unpack(got_ref[pl.ds(q, 1)])
    stacked = jnp.concatenate([own_panel[:, 0:32], own_panel[:, 32:64]], axis=0)
    ranks = jnp.concatenate([jnp.full_like(own_rank, -1), own_rank], axis=0)
    lane = iota((128, 128), 1)
    left = jnp.where(lane < 32, jnp.concatenate([stacked] * 4, axis=1), one(ranks == lane - 32))
    left = jnp.where(lane < 48, left, 0.0)
    left = jnp.transpose(left)
    pair_cls = jnp.concatenate([own_cls ^ l_ref[0], own_cls ^ l_ref[1]], axis=0)
    both = [jnp.concatenate([part[:, 0:32], part[:, 32:64]], axis=0) for part in parts]
    spread = [
        jnp.where(label == (pair_cls ^ xs[n]), jnp.concatenate([both[n]] * 4, axis=1), 0.0) for n in range(8)
    ]
    sums = dot3(split(left[0:32]), split(jnp.concatenate(spread, axis=1)))
    seconds = dot2(left[32:48].astype(BF16), split(jnp.concatenate(both, axis=1)))
    spots, numbers = places(row_ref)
    order = dot(spots, numbers, NT).astype(BF16)
    for i in range(2):
        rows = jnp.concatenate([sums[:, 128 * n : 128 * n + 128] for n in range(4 * i, 4 * i + 4)], axis=0)
        by_spot = dot2(order, split(rows), NT).reshape(16, RANKS, 128)
        out_ref[:, i, 64 : 64 + RANKS, :] = by_spot + seconds[None, :, 128 * i : 128 * i + 128]
        out_ref[:, i, 0:64, :] = jnp.broadcast_to(
            jnp.concatenate(firsts[4 * i : 4 * i + 4], axis=1)[None], (16, 64, 128)
        )


def ladder_kernel(row_ref, col_ref, got_ref, mid_ref, i_ref, j_ref, l_ref, pos_ref, out_ref):
    p, q = pos_ref[0], pos_ref[1]
    cls = row_ref[CLS : CLS + 1, :]
    number = row_ref[NUM : NUM + 1, :]
    label = row_ref[LAB : LAB + 1, 0:128]
    bits = row_ref[BITS : BITS + 1, 0:1]
    label_col = col_ref[0:128, LAB : LAB + 1]
    width = cls.shape[1]
    turned = jnp.transpose(unpack(got_ref[...]))
    full = [
        jnp.where(label_col == (cls ^ l_ref[n]), jnp.concatenate([turned[32 * n : 32 * n + 32]] * 4, axis=0), 0.0)
        for n in range(2)
    ]
    full = split(jnp.concatenate(full + [one(number == iota((128, width), 0))], axis=0))
    mids = [mid_ref[:, i, 0:64, :].reshape(width, 128) for i in range(2)]
    core = dot3(full, split(jnp.concatenate(mids, axis=1)))
    spots, numbers = places(row_ref)
    order = dot(numbers, spots, NT).astype(BF16)
    own_panel = unpack(got_ref[pl.ds(q, 1)])
    own_slot = own(col_ref, q, SLOT)
    own_rank = own(col_ref, q, RANK)
    own_cls = jnp.concatenate([own(col_ref, q, CLS)] * 4, axis=0)
    lane = iota((64, 128), 1)
    first_tile = jnp.concatenate([own_panel[:, 0:32]] * 4, axis=1)
    second_tile = jnp.concatenate([own_panel[:, 32:64]] * 4, axis=1)
    slot_tile = one(own_slot == (lane & 31))
    rank_pick = one(own_rank == lane).astype(BF16)
    lane_row = iota((1, 128), 1) >> 5
    results = []
    for i in range(2):
        xs = [i_ref[i] ^ j_ref[p * 4 + j] for j in range(4)]
        x_lane = jnp.zeros((1, 128), I32)
        x_row = jnp.zeros((256, 1), I32)
        for j in range(4):
            x_lane = jnp.where(lane_row == j, xs[j], x_lane)
            x_row = jnp.where((iota((256, 1), 0) >> 6) == j, xs[j], x_row)
        odd_lane = parity(x_lane & bits) == 1
        odd = [parity(bits & xs[j]) == 1 for j in range(4)]

        def blocks(tiles):
            return split(
                jnp.concatenate([jnp.where((lane >> 5) == j, tiles[j], 0.0) for j in range(4)], axis=0)
            )

        late = mid_ref[:, i, 64 : 64 + RANKS, :]
        total = jnp.where(odd_lane, 0.0, jnp.sum(late, axis=0))
        late = jnp.where(odd_lane, late.reshape(16 * RANKS, 128), 0.0)
        lanes = slice(128 * i, 128 * i + 128)
        pick = core[256:384, lanes]
        pick2 = jnp.where(odd_lane, dot2(order, split(late)), pick)
        t1 = dot3(blocks([jnp.where(odd[j], slot_tile, first_tile) for j in range(4)]), split(pick), NT)
        t2 = dot3(blocks([jnp.where(odd[j], slot_tile, second_tile) for j in range(4)]), split(pick2), NT)
        t3 = dot3(blocks([first_tile] * 4), split(core[0:128, lanes]), NT)
        t3 = t3 + dot3(blocks([second_tile] * 4), split(core[128:256, lanes]), NT)
        total = jnp.concatenate([total, jnp.zeros((128 - RANKS, 128), F32)], axis=0)
        total = dot2(rank_pick, split(total))
        spread = [jnp.concatenate([total[:, 32 * j : 32 * j + 32]] * 4, axis=1) for j in range(4)]
        t3 = t3 + jnp.concatenate(spread, axis=0)
        goal = own_cls ^ x_row
        t1 = jnp.where(label == (goal ^ l_ref[0]), t1, 0.0)
        t2 = jnp.where(label == (goal ^ l_ref[1]), t2, 0.0)
        t3 = jnp.where(label == goal, t3, 0.0)
        results.append(jnp.concatenate([t1, t2, t3], axis=1))
    result = dot3(split(jnp.concatenate(results, axis=0)), full)
    for n in range(8):
        out_ref[n // 4, n % 4] = result[64 * n : 64 * n + 64]


VMEM = pl.BlockSpec(memory_space=pltpu.VMEM)
SMEM = pl.BlockSpec(memory_space=pltpu.SMEM)
PARAMS = pltpu.CompilerParams(vmem_limit_bytes=48 * 1024 * 1024)


def shape(*dims, dtype=F32):
    return jax.ShapeDtypeStruct(dims, dtype)


def compact(row, col, amplitudes, chol, irrep_i, irrep_j, irrep_l, pos):
    panel = pl.pallas_call(
        panel_kernel,
        out_shape=shape(16, 32, 128),
        in_specs=[VMEM, VMEM, VMEM, SMEM, SMEM],
        out_specs=VMEM,
        compiler_params=PARAMS,
        name="panel_slots",
    )(row, col, chol, irrep_l, pos)
    panel = lax.all_to_all(panel, "ja", split_axis=0, concat_axis=0, tiled=True)
    mid = pl.pallas_call(
        half_kernel,
        out_shape=shape(16, 2, 64 + RANKS, 128),
        in_specs=[VMEM] * 4 + [SMEM] * 4,
        out_specs=VMEM,
        scratch_shapes=[pltpu.VMEM((512, 1024), BF16), pltpu.VMEM((512, 1024), BF16)],
        compiler_params=PARAMS,
        name="half_slots",
    )(row, col, amplitudes, panel, irrep_i, irrep_j, irrep_l, pos)
    mid = lax.all_to_all(mid, "aa", split_axis=0, concat_axis=0, tiled=True)
    return pl.pallas_call(
        ladder_kernel,
        out_shape=shape(*amplitudes.shape),
        in_specs=[VMEM] * 4 + [SMEM] * 4,
        out_specs=VMEM,
        compiler_params=PARAMS,
        name="ladder_slots",
    )(row, col, panel, mid, irrep_i, irrep_j, irrep_l, pos)


def panel_rows(half_ref, other_ref, core, high_ref, low_ref):
    for k in range(half_ref.shape[0]):
        for part, ref in ((core, half_ref), (1 - core, other_ref)):
            rows = pl.ds(pl.multiple_of((2 * k + part) * 64, 64), 64)
            high_ref[rows, :], low_ref[rows, :] = split(ref[k])


def dense_half_kernel(
    row_ref, col_ref, amp_ref, half_ref, other_ref, i_ref, j_ref, pos_ref, out_ref, ph_ref, pl_ref, high_ref, low_ref
):
    p, q = pos_ref[0], pos_ref[1]
    panel_rows(half_ref, other_ref, p & 1, ph_ref, pl_ref)
    cls = row_ref[CLS : CLS + 1, :]
    own_cls = own(col_ref, q, CLS)
    for n in range(8):
        kept = jnp.where((own_cls ^ cls) == (i_ref[n // 4] ^ j_ref[p * 4 + n % 4]), amp_ref[n // 4, n % 4], 0.0)
        high_ref[64 * n : 64 * n + 64, :], low_ref[64 * n : 64 * n + 64, :] = split(kept)
    result = dot3((ph_ref[...], pl_ref[...]), (high_ref[...], low_ref[...]), NT)
    out_ref[...] = result.reshape(out_ref.shape)


def dense_ladder_kernel(
    row_ref, col_ref, mid_ref, half_ref, other_ref, i_ref, j_ref, pos_ref, out_ref, ph_ref, pl_ref, high_ref, low_ref
):
    p, q = pos_ref[0], pos_ref[1]
    panel_rows(half_ref, other_ref, p & 1, ph_ref, pl_ref)
    first = iota((64, 128), 1) < 64
    for n in range(8):
        lanes = slice(128 * (n // 2), 128 * (n // 2) + 128)
        for s in range(0, 16, 2):
            a, b = mid_ref[s, :, lanes], mid_ref[s + 1, :, lanes]
            both = jnp.where(first, a, jnp.roll(b, 64, axis=1)) if n % 2 == 0 else jnp.where(first, jnp.roll(a, 64, axis=1), b)
            place = (slice(64 * n, 64 * n + 64), slice(64 * s, 64 * s + 128))
            high_ref[place], low_ref[place] = split(both)
    result = dot3((high_ref[...], low_ref[...]), (ph_ref[...], pl_ref[...]))
    pair_cls = own(col_ref, q, CLS) ^ row_ref[CLS : CLS + 1, :]
    for n in range(8):
        x = i_ref[n // 4] ^ j_ref[p * 4 + n % 4]
        out_ref[n // 4, n % 4] = jnp.where(pair_cls == x, result[64 * n : 64 * n + 64], 0.0)


CORES = [[2 * k + core for k in range(8)] for core in (0, 1)]


def dense(row, col, amplitudes, panel, irrep_i, irrep_j, pos):
    half = jnp.broadcast_to(panel[None], (8, *panel.shape))
    half = lax.all_to_all(half, "ja", split_axis=0, concat_axis=0, tiled=True, axis_index_groups=CORES)
    other = lax.ppermute(half, "ja", [(n, n ^ 1) for n in range(16)])
    halves = [pltpu.VMEM((1024, 1024), BF16)] * 2 + [pltpu.VMEM((512, 1024), BF16)] * 2
    mid = pl.pallas_call(
        dense_half_kernel,
        out_shape=shape(16, 64, 512),
        in_specs=[VMEM] * 5 + [SMEM] * 3,
        out_specs=VMEM,
        scratch_shapes=halves,
        compiler_params=PARAMS,
        name="half_dense",
    )(row, col, amplitudes, half, other, irrep_i, irrep_j, pos)
    mid = lax.all_to_all(mid, "aa", split_axis=0, concat_axis=0, tiled=True)
    return pl.pallas_call(
        dense_ladder_kernel,
        out_shape=shape(*amplitudes.shape),
        in_specs=[VMEM] * 5 + [SMEM] * 3,
        out_specs=VMEM,
        scratch_shapes=halves,
        compiler_params=PARAMS,
        name="ladder_dense",
    )(row, col, mid, half, other, irrep_i, irrep_j, pos)


def local(amplitudes, chol, irrep_i, irrep_j, irrep_v, irrep_l):
    pos = jnp.stack([lax.axis_index("ja"), lax.axis_index("aa")]).astype(I32)
    width = irrep_v.shape[0]
    row, col = pl.pallas_call(
        table_kernel,
        out_shape=(shape(8, width, dtype=I32), shape(width, 128, dtype=I32)),
        in_specs=[VMEM, SMEM],
        out_specs=(VMEM, VMEM),
        compiler_params=PARAMS,
        name="orbital_table",
    )(irrep_v.reshape(1, width), irrep_l)
    height = chol.shape[1]

    def panels():
        own_rows = lax.dynamic_slice_in_dim(irrep_v, pos[0] * height, height)
        pair = own_rows[:, None] ^ irrep_v[None, :]
        return [jnp.where(pair == irrep_l[n], chol[n], 0.0) for n in range(2)]

    def run(panel):
        return dense(row, col, amplitudes, panel, irrep_i, irrep_j, pos)

    def together():
        first, second = panels()
        return run(first + second)

    def apart():
        first, second = panels()
        return run(first) + run(second)

    return lax.switch(
        jnp.where(row[FLAG, 0] == 1, 0, jnp.where(irrep_l[0] != irrep_l[1], 1, 2)),
        [
            lambda: compact(row, col, amplitudes, chol, irrep_i, irrep_j, irrep_l, pos),
            together,
            apart,
        ],
    )


def solution(mesh):
    in_specs = (P(None, "ja", "aa", None), P(None, "ja", None), P(), P(), P(), P())
    out_specs = P(None, "ja", "aa", None)
    return jax.shard_map(local, mesh=mesh, in_specs=in_specs, out_specs=out_specs, check_vma=False)
```

profile of v0, /device:TPU:32, one launch (start us, length us, event | category | flops | bytes accessed | tf_op | source)
XLA Modules:
  0.0 74.4 jit_solution(6511905787654837047)
XLA Ops:
  0.0 0.1 pad_add_fusion
  0.1 1.3 %fusion.2 = (s32[1]{0:T(128)}, s32[1]{0:T(128)}) fusion(s32[2]{0:T(128)} %l_ref.1), kind=kLoop, calls=%fused_computation.10 | loop fusion | bytes 16 | tf_op jit(solution)/shard_map/slice | solution.py:400
  2.7 1.6 %orbital_table.1 = (s32[8,1024]{1,0:T(8,128)S(1)}, s32[1024,128]{1,0:T(8,128)S(1)}) custom-call(s32[1,1024]{1,0:T(1,128)} %bitcast.15, s32[2]{0:T(128)} %l_ref.1), custom_call_target="tpu_custom_call" | custom-call | tf_op jit(solution)/shard_map/orbital_table/pallas_call | solution.py:373
  4.3 0.5 slice.33
  5.5 68.9 %conditional.1 = (f32[2,4,64,1024]{3,2,1,0:T(8,128)}) conditional(s32[]{:T(128)} %clamp.3, (s32[8,1024]{1,0:T(8,128)S(1)}, s32[1024,128]{1,0:T(8,128)S(1)}, f32[2,64,1024]{2,1,0:T(8,128)}, s32[2]{0:T(128)}, s32[2]{0:T(128)S(1)}, /*index=5*/f32[2,4,64,1024]{3,2,1,0:T(8,128)}, s32[2]{0:T(128)}, s32[64]{0:T(128)}) %tuple.14, ...), branch_computations={%region_0.1_spmd, %region_1.2_spmd, %region_2.3_spmd} | conditional | flops 851972 | bytes 102242560 | solution.py:399
  5.5 1.6 %panel_slots.1 = f32[16,32,128]{2,1,0:T(8,128)S(1)} custom-call(s32[8,1024]{1,0:T(8,128)S(1)} %get-tuple-element.64.row_ref, s32[1024,128]{1,0:T(8,128)S(1)} %get-tuple-element.66.col_ref, f32[2,64,1024]{2,1,0:T(8,128)} %get-tuple-element.67.chol_ref, s32[2]{0:T(128)} %get-tuple-element.68.l_ref, s32[2]{0:T(128)S(1)} %get-tuple-element.69.pos_ref), custom_call_target="tpu_custom_call" | custom-call | tf_op jit(solution)/shard_map/cond/branch_0_fun/panel_slots/pallas_call | solution.py:271
  7.1 16.2 %all_to_all.32.got_ref = f32[16,32,128]{2,1,0:T(8,128)S(1)} all-to-all(f32[16,32,128]{2,1,0:T(8,128)S(1)} %panel_slots.1), channel_id=1, replica_groups=mesh['ja'=16,'aa'=16] {'ja'}, dimensions={0} | all-to-all | bytes 524288 | tf_op jit(solution)/shard_map/cond/branch_0_fun/all_to_all | solution.py:279
  23.3 3.6 %half_slots.1 = f32[16,2,80,128]{3,2,1,0:T(8,128)S(1)} custom-call(s32[8,1024]{1,0:T(8,128)S(1)} %get-tuple-element.64.row_ref, s32[1024,128]{1,0:T(8,128)S(1)} %get-tuple-element.66.col_ref, f32[2,4,64,1024]{3,2,1,0:T(8,128)} %get-tuple-element.70.amp_ref, f32[16,32,128]{2,1,0:T(8,128)S(1)} %all_to_all.32.got_ref, s32[2]{0:T(128)} %get-tuple-element.71.i_ref, ...), custom_call_target="tpu_custom_call" | custom-call | tf_op jit(solution)/shard_map/cond/branch_0_fun/half_slots/pallas_call | solution.py:280
  27.0 0.0 copy-start.8
  27.0 0.0 copy-start.9
  27.0 0.0 copy-start.12
  27.0 41.3 %all_to_all.33.mid_ref = f32[16,2,80,128]{3,2,1,0:T(8,128)S(1)} all-to-all(f32[16,2,80,128]{3,2,1,0:T(8,128)S(1)} %half_slots.1), channel_id=1, replica_groups=mesh['ja'=16,'aa'=16] {'aa'}, dimensions={0} | all-to-all | bytes 2621440 | tf_op jit(solution)/shard_map/cond/branch_0_fun/all_to_all | solution.py:289
  68.3 0.0 copy-done.8
  68.3 0.0 copy-done.9
  68.3 0.0 copy-done.12
  68.3 6.2 %ladder_slots.1 = f32[2,4,64,1024]{3,2,1,0:T(8,128)} custom-call(s32[8,1024]{1,0:T(8,128)S(1)} %get-tuple-element.64.row_ref, s32[1024,128]{1,0:T(8,128)S(1)} %get-tuple-element.66.col_ref, f32[16,32,128]{2,1,0:T(8,128)S(1)} %all_to_all.32.got_ref, f32[16,2,80,128]{3,2,1,0:T(8,128)S(1)} %all_to_all.33.mid_ref, s32[2]{0:T(128)S(1)} %copy-done.9, ...), custom_call_target="tpu_custom_call" | custom-call | tf_op jit(solution)/shard_map/cond/branch_0_fun/ladder_slots/pallas_call | solution.py:290
Async XLA Ops:
  27.0 41.3 %copy-start.8 = (s32[2]{0:T(128)S(1)}, s32[2]{0:T(128)}, u32[]{:S(2)}) copy-start(s32[2]{0:T(128)} %get-tuple-element.68.l_ref) | copy-start | bytes 28 | tf_op jit(solution)/shard_map/cond
  27.0 41.3 %copy-start.9 = (s32[2]{0:T(128)S(1)}, s32[2]{0:T(128)}, u32[]{:S(2)}) copy-start(s32[2]{0:T(128)} %get-tuple-element.71.i_ref) | copy-start | bytes 28 | tf_op jit(solution)/shard_map/cond
  27.0 41.3 %copy-start.12 = (s32[64]{0:T(128)S(1)}, s32[64]{0:T(128)}, u32[]{:S(2)}) copy-start(s32[64]{0:T(128)} %get-tuple-element.72.j_ref) | copy-start | bytes 772 | tf_op jit(solution)/shard_map/cond
where the time goes:
time: 74.7 us; the launch traced here: 74.4 us
  blocking collectives  57.5 us (77%)
  Pallas kernels  13 us (17%)
  between operations  2.02 us (3%)
  local copies, waits for them, and re-layouts  1.86 us (2%)
    all_to_all x1, blocking collectives, compact(): mid = lax.all_to_all(mid, 'aa', split_axis=0, concat_axis=0, tiled=True)  41.3 us
    all_to_all x1, blocking collectives, compact(): panel = lax.all_to_all(panel, 'ja', split_axis=0, concat_axis=0, tiled=True)  16.2 us
    pallas_call x1, Pallas kernels, compact(): pl.pallas_call(ladder_kernel, out_shape=shape(*amplitudes.shape), in_spec...  6.16 us
    pallas_call x1, Pallas kernels, compact(): pl.pallas_call(half_kernel, out_shape=shape(16, 2, 64 + RANKS, 128), in_s...  3.65 us
    pallas_call x1, Pallas kernels, compact(): pl.pallas_call(panel_kernel, out_shape=shape(16, 32, 128), in_specs=[VMEM...  1.59 us
    pallas_call x1, Pallas kernels, local(): pl.pallas_call(table_kernel, out_shape=(shape(8, width, dtype=I32), shape...  1.57 us

commit v1 on v0

--- a/solution.py
+++ b/solution.py
@@ -10,7 +10,7 @@
 NT = (((1,), (1,)), ((), ()))
 SLOTS = 32
 RANKS = 16
-CLS, NUM, SLOT, SPOT, LAB, RANK, FLAG, BITS = range(8)
+CLS, NUM, SLOT, SPOT, LAB, RANK, BRANCH, BITS = range(8)
 
 
 def iota(shape, dim):
@@ -43,7 +43,7 @@
     return dot(a, b[0], dims) + dot(a, b[1], dims)
 
 
-def table_kernel(irrep_ref, l_ref, row_ref, col_ref):
+def table_kernel(irrep_ref, chol_ref, i_ref, l_ref, pos_ref, row_ref, col_ref, out_ref):
     cls = irrep_ref[...]
     width = cls.shape[1]
     chunks = width // 128
@@ -73,8 +73,11 @@
     good = (largest <= SLOTS) & (fullest <= RANKS)
     for n in range(l_ref.shape[0]):
         good = good & (parity(bits_col & l_ref[n]) == 1)
-    pick = jnp.min(jnp.where(good, cand[:, 0:1].astype(F32), 99.0), axis=0, keepdims=True).astype(I32)
-    bits, side = pick >> 1, pick & 1
+    rank = cand[:, 0:1] + jnp.where(parity(bits_col & (i_ref[0] ^ i_ref[1])) == 1, 0, 16)
+    pick = jnp.min(jnp.where(good, rank.astype(F32), 99.0), axis=0, keepdims=True).astype(I32)
+    dense_branch = jnp.where(l_ref[0] != l_ref[1], 2, 3)
+    branch = jnp.where(pick < 16, 0, jnp.where(pick < 32, 1, dense_branch))
+    bits, side = (pick & 15) >> 1, pick & 1
     small = parity(bits & cls) == side
     group = jnp.zeros_like(cls)
     label = jnp.zeros_like(cls)
@@ -100,7 +103,7 @@
             jnp.where(small, (iota((1, width), 1) >> 6) * RANKS + rank, none),
             label,
             jnp.where(small, rank, none),
-            jnp.broadcast_to(jnp.where(pick < 99, 1, 0), cls.shape),
+            jnp.broadcast_to(branch, cls.shape),
             jnp.broadcast_to(bits, cls.shape),
         ],
         axis=0,
@@ -110,13 +113,14 @@
     for k in range(chunks):
         tile = jnp.concatenate([table[:, 128 * k : 128 * k + 128], jnp.zeros((120, 128), F32)], axis=0)
         col_ref[128 * k : 128 * k + 128, :] = jnp.transpose(tile).astype(I32)
+    panel_slots(row_ref, col_ref, chol_ref, l_ref, pos_ref, out_ref)
 
 
 def own(col_ref, block, field):
     return col_ref[pl.ds(pl.multiple_of(block * 64, 64), 64), field : field + 1]
 
 
-def panel_kernel(row_ref, col_ref, chol_ref, l_ref, pos_ref, out_ref):
+def panel_slots(row_ref, col_ref, chol_ref, l_ref, pos_ref, out_ref):
     cls = row_ref[CLS : CLS + 1, :]
     slot = row_ref[SLOT : SLOT + 1, :]
     own_cls = own(col_ref, pos_ref[0], CLS)
@@ -143,51 +147,6 @@
     spots = one(spot == iota((16 * RANKS, width), 0)).astype(BF16)
     numbers = one(number == iota((4 * SLOTS, width), 0)).astype(BF16)
     return spots, numbers
-
-
-def half_kernel(row_ref, col_ref, amp_ref, got_ref, i_ref, j_ref, l_ref, pos_ref, out_ref, high_ref, low_ref):
-    p, q = pos_ref[0], pos_ref[1]
-    cls = row_ref[CLS : CLS + 1, :]
-    label = row_ref[LAB : LAB + 1, 0:128]
-    own_cls = own(col_ref, q, CLS)
-    own_small = own(col_ref, q, NUM) >= 0
-    own_rank = own(col_ref, q, RANK)
-    xs = [i_ref[n // 4] ^ j_ref[p * 4 + n % 4] for n in range(8)]
-    for n in range(8):
-        kept = jnp.where((own_cls ^ cls) == xs[n], amp_ref[n // 4, n % 4], 0.0)
-        high_ref[64 * n : 64 * n + 64, :], low_ref[64 * n : 64 * n + 64, :] = split(kept)
-    panel = unpack(got_ref[...])
-    lane = iota(panel.shape, 1)
-    slot = col_ref[:, SLOT : SLOT + 1]
-    weights = jnp.where(lane < 64, panel, one(slot == lane - 64))
-    wh, wl = split(weights)
-    first = dot(high_ref[...], jnp.concatenate([wh, wl], axis=1))
-    half = first[:, 0:128] + first[:, 128:256] + dot(low_ref[...], wh)
-    parts = [half[64 * n : 64 * n + 64] for n in range(8)]
-    firsts = [part[:, 64:96] + jnp.where(own_small, part[:, 0:32], 0.0) for part in parts]
-    own_panel = unpack(got_ref[pl.ds(q, 1)])
-    stacked = jnp.concatenate([own_panel[:, 0:32], own_panel[:, 32:64]], axis=0)
-    ranks = jnp.concatenate([jnp.full_like(own_rank, -1), own_rank], axis=0)
-    lane = iota((128, 128), 1)
-    left = jnp.where(lane < 32, jnp.concatenate([stacked] * 4, axis=1), one(ranks == lane - 32))
-    left = jnp.where(lane < 48, left, 0.0)
-    left = jnp.transpose(left)
-    pair_cls = jnp.concatenate([own_cls ^ l_ref[0], own_cls ^ l_ref[1]], axis=0)
-    both = [jnp.concatenate([part[:, 0:32], part[:, 32:64]], axis=0) for part in parts]
-    spread = [
-        jnp.where(label == (pair_cls ^ xs[n]), jnp.concatenate([both[n]] * 4, axis=1), 0.0) for n in range(8)
-    ]
-    sums = dot3(split(left[0:32]), split(jnp.concatenate(spread, axis=1)))
-    seconds = dot2(left[32:48].astype(BF16), split(jnp.concatenate(both, axis=1)))
-    spots, numbers = places(row_ref)
-    order = dot(spots, numbers, NT).astype(BF16)
-    for i in range(2):
-        rows = jnp.concatenate([sums[:, 128 * n : 128 * n + 128] for n in range(4 * i, 4 * i + 4)], axis=0)
-        by_spot = dot2(order, split(rows), NT).reshape(16, RANKS, 128)
-        out_ref[:, i, 64 : 64 + RANKS, :] = by_spot + seconds[None, :, 128 * i : 128 * i + 128]
-        out_ref[:, i, 0:64, :] = jnp.broadcast_to(
-            jnp.concatenate(firsts[4 * i : 4 * i + 4], axis=1)[None], (16, 64, 128)
-        )
 
 
 def ladder_kernel(row_ref, col_ref, got_ref, mid_ref, i_ref, j_ref, l_ref, pos_ref, out_ref):
@@ -258,6 +217,156 @@
         out_ref[n // 4, n % 4] = result[64 * n : 64 * n + 64]
 
 
+def half_products(row_ref, col_ref, amp_ref, got_ref, i_ref, j_ref, pos_ref, high_ref, low_ref):
+    p, q = pos_ref[0], pos_ref[1]
+    cls = row_ref[CLS : CLS + 1, :]
+    own_cls = own(col_ref, q, CLS)
+    for n in range(8):
+        kept = jnp.where((own_cls ^ cls) == (i_ref[n // 4] ^ j_ref[p * 4 + n % 4]), amp_ref[n // 4, n % 4], 0.0)
+        high_ref[64 * n : 64 * n + 64, :], low_ref[64 * n : 64 * n + 64, :] = split(kept)
+    panel = unpack(got_ref[...])
+    lane = iota(panel.shape, 1)
+    slot = col_ref[:, SLOT : SLOT + 1]
+    wh, wl = split(jnp.where(lane < 64, panel, one(slot == lane - 64)))
+    first = dot(high_ref[...], jnp.concatenate([wh, wl], axis=1))
+    half = first[:, 0:128] + first[:, 128:256] + dot(low_ref[...], wh)
+    return [half[64 * n : 64 * n + 64] for n in range(8)]
+
+
+def left_factor(col_ref, got_ref, q):
+    own_rank = own(col_ref, q, RANK)
+    own_panel = unpack(got_ref[pl.ds(q, 1)])
+    stacked = jnp.concatenate([own_panel[:, 0:32], own_panel[:, 32:64]], axis=0)
+    ranks = jnp.concatenate([jnp.full_like(own_rank, -1), own_rank], axis=0)
+    lane = iota((128, 128), 1)
+    left = jnp.where(lane < 32, jnp.concatenate([stacked] * 4, axis=1), one(ranks == lane - 32))
+    return jnp.transpose(jnp.where(lane < 48, left, 0.0))
+
+
+def odd_even(row_ref, i_ref, j_ref, p):
+    bits = row_ref[BITS : BITS + 1, 0:1]
+    later = [parity(bits & (i_ref[1] ^ j_ref[p * 4 + j])) == 1 for j in range(4)]
+    xs = [[jnp.where(later[j], i_ref[i] ^ j_ref[p * 4 + j], i_ref[1 - i] ^ j_ref[p * 4 + j]) for j in range(4)] for i in (1, 0)]
+    return later, xs[0], xs[1]
+
+
+def half_kernel(row_ref, col_ref, amp_ref, got_ref, i_ref, j_ref, l_ref, pos_ref, out_ref, high_ref, low_ref):
+    p, q = pos_ref[0], pos_ref[1]
+    label = row_ref[LAB : LAB + 1, 0:128]
+    own_cls = own(col_ref, q, CLS)
+    own_small = own(col_ref, q, NUM) >= 0
+    xs = [i_ref[n // 4] ^ j_ref[p * 4 + n % 4] for n in range(8)]
+    parts = half_products(row_ref, col_ref, amp_ref, got_ref, i_ref, j_ref, pos_ref, high_ref, low_ref)
+    firsts = [part[:, 64:96] + jnp.where(own_small, part[:, 0:32], 0.0) for part in parts]
+    left = left_factor(col_ref, got_ref, q)
+    pair_cls = jnp.concatenate([own_cls ^ l_ref[0], own_cls ^ l_ref[1]], axis=0)
+    both = [jnp.concatenate([part[:, 0:32], part[:, 32:64]], axis=0) for part in parts]
+    spread = [
+        jnp.where(label == (pair_cls ^ xs[n]), jnp.concatenate([both[n]] * 4, axis=1), 0.0) for n in range(8)
+    ]
+    sums = dot3(split(left[0:32]), split(jnp.concatenate(spread, axis=1)))
+    seconds = dot2(left[32:48].astype(BF16), split(jnp.concatenate(both, axis=1)))
+    spots, numbers = places(row_ref)
+    order = dot(spots, numbers, NT).astype(BF16)
+    for i in range(2):
+        rows = jnp.concatenate([sums[:, 128 * n : 128 * n + 128] for n in range(4 * i, 4 * i + 4)], axis=0)
+        by_spot = dot2(order, split(rows), NT).reshape(16, RANKS, 128)
+        out_ref[:, i, 64 : 64 + RANKS, :] = by_spot + seconds[None, :, 128 * i : 128 * i + 128]
+        out_ref[:, i, 0:64, :] = jnp.broadcast_to(
+            jnp.concatenate(firsts[4 * i : 4 * i + 4], axis=1)[None], (16, 64, 128)
+        )
+
+
+def half_paired_kernel(row_ref, col_ref, amp_ref, got_ref, i_ref, j_ref, l_ref, pos_ref, out_ref, high_ref, low_ref):
+    p, q = pos_ref[0], pos_ref[1]
+    label = row_ref[LAB : LAB + 1, 0:128]
+    own_cls = own(col_ref, q, CLS)
+    own_small = own(col_ref, q, NUM) >= 0
+    parts = half_products(row_ref, col_ref, amp_ref, got_ref, i_ref, j_ref, pos_ref, high_ref, low_ref)
+    later, _, even_x = odd_even(row_ref, i_ref, j_ref, p)
+    odd = [jnp.where(later[j], parts[4 + j], parts[j]) for j in range(4)]
+    even = [jnp.where(later[j], parts[j], parts[4 + j]) for j in range(4)]
+    rows = jnp.concatenate([part[:, 64:96] + jnp.where(own_small, part[:, 0:32], 0.0) for part in odd], axis=1)
+    out_ref[:, 0:64, :] = jnp.broadcast_to(rows[None], (16, 64, 128))
+    left = left_factor(col_ref, got_ref, q)
+    firsts = jnp.concatenate([part[:, 64:96] for part in even], axis=1)
+    seconds = jnp.concatenate([part[:, 32:64] for part in odd], axis=1)
+    few = jnp.concatenate([firsts, seconds], axis=1)
+    few = dot2(left[32:48].astype(BF16), split(jnp.concatenate([few, few], axis=0)))
+    for k in range(2):
+        few_rows = few[None, :, 128 * k : 128 * k + 128]
+        out_ref[:, 64 + RANKS * k : 64 + RANKS * (k + 1), :] = jnp.broadcast_to(few_rows, (16, RANKS, 128))
+    pair_cls = jnp.concatenate([own_cls ^ l_ref[0], own_cls ^ l_ref[1]], axis=0)
+    spread = []
+    for j in range(4):
+        both = jnp.concatenate([even[j][:, 0:32], even[j][:, 32:64]], axis=0)
+        spread.append(jnp.where(label == (pair_cls ^ even_x[j]), jnp.concatenate([both] * 4, axis=1), 0.0))
+    sums = dot3(split(left[0:32]), split(jnp.concatenate(spread, axis=1)))
+    sums = jnp.concatenate([sums[:, 128 * j : 128 * j + 128] for j in range(4)], axis=0)
+    spots, numbers = places(row_ref)
+    order = dot(spots, numbers, NT).astype(BF16)
+    out_ref[:, 64 + 2 * RANKS : 64 + 3 * RANKS, :] = dot2(order, split(sums), NT).reshape(16, RANKS, 128)
+
+
+def ladder_paired_kernel(row_ref, col_ref, got_ref, mid_ref, i_ref, j_ref, l_ref, pos_ref, out_ref):
+    p, q = pos_ref[0], pos_ref[1]
+    cls = row_ref[CLS : CLS + 1, :]
+    number = row_ref[NUM : NUM + 1, :]
+    label = row_ref[LAB : LAB + 1, 0:128]
+    label_col = col_ref[0:128, LAB : LAB + 1]
+    width = cls.shape[1]
+    turned = jnp.transpose(unpack(got_ref[...]))
+    full = [
+        jnp.where(label_col == (cls ^ l_ref[n]), jnp.concatenate([turned[32 * n : 32 * n + 32]] * 4, axis=0), 0.0)
+        for n in range(2)
+    ]
+    full = split(jnp.concatenate(full + [one(number == iota((128, width), 0))], axis=0))
+    core = dot3(full, split(mid_ref[:, 0:64, :].reshape(width, 128)))
+    spots, numbers = places(row_ref)
+    order = dot(numbers, spots, NT).astype(BF16)
+    few = [mid_ref[:, 64 + RANKS * k : 64 + RANKS * (k + 1), :] for k in range(3)]
+    small_rows, second_rows = [dot2(order, split(few[k].reshape(16 * RANKS, 128))) for k in range(2)]
+    total = jnp.concatenate([jnp.sum(few[2], axis=0), jnp.zeros((128 - RANKS, 128), F32)], axis=0)
+    own_panel = unpack(got_ref[pl.ds(q, 1)])
+    own_slot = own(col_ref, q, SLOT)
+    own_rank = own(col_ref, q, RANK)
+    own_cls = own(col_ref, q, CLS)
+    lane = iota((64, 128), 1)
+
+    def blocks(tile):
+        return split(jnp.concatenate([jnp.where((lane >> 5) == j, tile, 0.0) for j in range(4)], axis=0))
+
+    first = blocks(jnp.concatenate([own_panel[:, 0:32]] * 4, axis=1))
+    second = blocks(jnp.concatenate([own_panel[:, 32:64]] * 4, axis=1))
+    slots = blocks(one(own_slot == (lane & 31)))[0]
+    total = dot2(one(own_rank == lane).astype(BF16), split(total))
+    total = [jnp.concatenate([total[:, 32 * j : 32 * j + 32]] * 4, axis=1) for j in range(4)]
+    odd = [
+        dot2(slots, split(core[256:384]), NT),
+        dot2(slots, split(second_rows), NT),
+        dot3(first, split(core[0:128]), NT) + dot3(second, split(core[128:256]), NT),
+    ]
+    small_rows = split(small_rows)
+    even = [dot3(first, small_rows, NT), dot3(second, small_rows, NT), jnp.concatenate(total, axis=0)]
+    later, odd_x, even_x = odd_even(row_ref, i_ref, j_ref, p)
+    rows = [None] * 8
+    for j in range(4):
+        kinds = []
+        for parts, x in ((odd, odd_x[j]), (even, even_x[j])):
+            goal = own_cls ^ x
+            labels = (goal ^ l_ref[0], goal ^ l_ref[1], goal)
+            kinds.append(
+                jnp.concatenate(
+                    [jnp.where(label == labels[k], parts[k][64 * j : 64 * j + 64], 0.0) for k in range(3)], axis=1
+                )
+            )
+        rows[j] = jnp.where(later[j], kinds[1], kinds[0])
+        rows[4 + j] = jnp.where(later[j], kinds[0], kinds[1])
+    result = dot3(split(jnp.concatenate(rows, axis=0)), full)
+    for n in range(8):
+        out_ref[n // 4, n % 4] = result[64 * n : 64 * n + 64]
+
+
 VMEM = pl.BlockSpec(memory_space=pltpu.VMEM)
 SMEM = pl.BlockSpec(memory_space=pltpu.SMEM)
 PARAMS = pltpu.CompilerParams(vmem_limit_bytes=48 * 1024 * 1024)
@@ -267,19 +376,11 @@
     return jax.ShapeDtypeStruct(dims, dtype)
 
 
-def compact(row, col, amplitudes, chol, irrep_i, irrep_j, irrep_l, pos):
-    panel = pl.pallas_call(
-        panel_kernel,
-        out_shape=shape(16, 32, 128),
-        in_specs=[VMEM, VMEM, VMEM, SMEM, SMEM],
-        out_specs=VMEM,
-        compiler_params=PARAMS,
-        name="panel_slots",
-    )(row, col, chol, irrep_l, pos)
+def compact(kernels, middle, row, col, panel, amplitudes, irrep_i, irrep_j, irrep_l, pos):
     panel = lax.all_to_all(panel, "ja", split_axis=0, concat_axis=0, tiled=True)
     mid = pl.pallas_call(
-        half_kernel,
-        out_shape=shape(16, 2, 64 + RANKS, 128),
+        kernels[0],
+        out_shape=shape(16, *middle, 128),
         in_specs=[VMEM] * 4 + [SMEM] * 4,
         out_specs=VMEM,
         scratch_shapes=[pltpu.VMEM((512, 1024), BF16), pltpu.VMEM((512, 1024), BF16)],
@@ -288,7 +389,7 @@
     )(row, col, amplitudes, panel, irrep_i, irrep_j, irrep_l, pos)
     mid = lax.all_to_all(mid, "aa", split_axis=0, concat_axis=0, tiled=True)
     return pl.pallas_call(
-        ladder_kernel,
+        kernels[1],
         out_shape=shape(*amplitudes.shape),
         in_specs=[VMEM] * 4 + [SMEM] * 4,
         out_specs=VMEM,
@@ -370,14 +471,14 @@
 def local(amplitudes, chol, irrep_i, irrep_j, irrep_v, irrep_l):
     pos = jnp.stack([lax.axis_index("ja"), lax.axis_index("aa")]).astype(I32)
     width = irrep_v.shape[0]
-    row, col = pl.pallas_call(
+    row, col, slots = pl.pallas_call(
         table_kernel,
-        out_shape=(shape(8, width, dtype=I32), shape(width, 128, dtype=I32)),
-        in_specs=[VMEM, SMEM],
-        out_specs=(VMEM, VMEM),
+        out_shape=(shape(8, width, dtype=I32), shape(width, 128, dtype=I32), shape(16, 32, 128)),
+        in_specs=[VMEM, VMEM, SMEM, SMEM, SMEM],
+        out_specs=(VMEM, VMEM, VMEM),
         compiler_params=PARAMS,
         name="orbital_table",
-    )(irrep_v.reshape(1, width), irrep_l)
+    )(irrep_v.reshape(1, width), chol, irrep_i, irrep_l, pos)
     height = chol.shape[1]
 
     def panels():
@@ -396,10 +497,12 @@
         first, second = panels()
         return run(first) + run(second)
 
+    few = (row, col, slots, amplitudes, irrep_i, irrep_j, irrep_l, pos)
     return lax.switch(
-        jnp.where(row[FLAG, 0] == 1, 0, jnp.where(irrep_l[0] != irrep_l[1], 1, 2)),
+        row[BRANCH, 0],
         [
-            lambda: compact(row, col, amplitudes, chol, irrep_i, irrep_j, irrep_l, pos),
+            lambda: compact((half_paired_kernel, ladder_paired_kernel), (64 + 3 * RANKS,), *few),
+            lambda: compact((half_kernel, ladder_kernel), (2, 64 + RANKS), *few),
             together,
             apart,
         ],

time: 74.7 us -> 61.6 us (0.82)
  blocking collectives: 57.5 us -> 48.4 us
  between operations: 2.02 us -> 0.66 us
  local copies, waits for them, and re-layouts: 1.86 us -> 0.53 us
  Pallas kernels: 13 us -> 11.7 us
    all_to_all x1, blocking collectives: 41.3 us -> 32.2 us  [compact(): mid = lax.all_to_all(mid, 'aa', split_axis=0, concat_axis=0, tiled=True)]
    pallas_call x3 -> x2, Pallas kernels: 11.4 us -> 9.29 us  [the longest x1 5.94 us: compact(): pl.pallas_call(kernels[1], out_shape=shape(*amplitudes.shape), in_specs=[...]
    slice x2 -> x1, local copies, waits for them, and re-layouts: 1.84 us -> 0.51 us  [local(): row[BRANCH, 0]]
    pallas_call x1, Pallas kernels: 1.57 us -> 2.42 us  [local(): pl.pallas_call(table_kernel, out_shape=(shape(8, width, dtype=I32), shape...]
where the time goes in v1:
time: 61.6 us; the launch traced here: 61.4 us
  blocking collectives  48.4 us (79%)
  Pallas kernels  11.7 us (19%)
  between operations  0.66 us (1%)
    all_to_all x1, blocking collectives, compact(): mid = lax.all_to_all(mid, 'aa', split_axis=0, concat_axis=0, tiled=True)  32.2 us
    all_to_all x1, blocking collectives, compact(): panel = lax.all_to_all(panel, 'ja', split_axis=0, concat_axis=0, tiled=True)  16.2 us
    pallas_call x1, Pallas kernels, compact(): pl.pallas_call(kernels[1], out_shape=shape(*amplitudes.shape), in_specs=[...  5.94 us
    pallas_call x1, Pallas kernels, compact(): pl.pallas_call(kernels[0], out_shape=shape(16, *middle, 128), in_specs=[V...  3.36 us
    pallas_call x1, Pallas kernels, local(): pl.pallas_call(table_kernel, out_shape=(shape(8, width, dtype=I32), shape...  2.42 us

profile of v1, /device:TPU:32, one launch (start us, length us, event | category | flops | bytes accessed | tf_op | source)
XLA Modules:
  0.0 61.4 jit_solution(7578107235423915409)
XLA Ops:
  0.0 0.1 pad_add_fusion.pos_ref
  0.1 2.4 %orbital_table.1 = (s32[8,1024]{1,0:T(8,128)S(1)}, s32[1024,128]{1,0:T(8,128)S(1)}, f32[16,32,128]{2,1,0:T(8,128)S(1)}) custom-call(s32[1,1024]{1,0:T(1,128)} %bitcast.14, f32[2,64,1024]{2,1,0:T(8,128)} %chol_ref.1, s32[2]{0:T(128)} %i_ref.1, s32[2]{0:T(128)} %l_ref.1, s32[2]{0:T(128)S(1)} %pad_add_fusion.pos_ref), custom_call_target="tpu_custom_call" | custom-call | tf_op jit(solution)/shard_map/orbital_table/pallas_call | solution.py:474
  2.5 0.5 slice.27
  3.7 57.8 %conditional.1 = (f32[2,4,64,1024]{3,2,1,0:T(8,128)}) conditional(s32[]{:T(128)} %bitcast.10, (f32[16,32,128]{2,1,0:T(8,128)S(1)}, s32[8,1024]{1,0:T(8,128)S(1)}, s32[1024,128]{1,0:T(8,128)S(1)}, f32[2,4,64,1024]{3,2,1,0:T(8,128)}, s32[2]{0:T(128)}, /*index=5*/s32[64]{0:T(128)}, s32[2]{0:T(128)}, ...), branch_computations={%region_0.0_spmd, %region_1.0_spmd, %region_2.3_spmd, %region_3.4_... | conditional | flops 851972 | bytes 102242560 | solution.py:501
  3.7 16.2 %all_to_all.40.got_ref = f32[16,32,128]{2,1,0:T(8,128)S(1)} all-to-all(f32[16,32,128]{2,1,0:T(8,128)S(1)} %get-tuple-element.84), channel_id=1, replica_groups=mesh['ja'=16,'aa'=16] {'ja'}, dimensions={0} | all-to-all | bytes 524288 | tf_op jit(solution)/shard_map/cond/branch_0_fun/all_to_all | solution.py:380
  19.9 0.0 copy-start.8
  19.9 0.0 copy-start.12
  19.9 0.0 copy-start.16
  19.9 3.4 %half_slots.2 = f32[16,112,128]{2,1,0:T(8,128)S(1)} custom-call(s32[8,1024]{1,0:T(8,128)S(1)} %get-tuple-element.80.row_ref, s32[1024,128]{1,0:T(8,128)S(1)} %get-tuple-element.82.col_ref, f32[2,4,64,1024]{3,2,1,0:T(8,128)} %get-tuple-element.85.amp_ref, f32[16,32,128]{2,1,0:T(8,128)S(1)} %all_to_all.40.got_ref, s32[2]{0:T(128)} %get-tuple-element.86.i_ref, ...), custom_call_target="tpu_custom_call" | custom-call | tf_op jit(solution)/shard_map/cond/branch_0_fun/half_slots/pallas_call | solution.py:381
  23.3 32.2 %all_to_all.41.mid_ref = f32[16,112,128]{2,1,0:T(8,128)S(1)} all-to-all(f32[16,112,128]{2,1,0:T(8,128)S(1)} %half_slots.2), channel_id=1, replica_groups=mesh['ja'=16,'aa'=16] {'aa'}, dimensions={0} | all-to-all | bytes 1835008 | tf_op jit(solution)/shard_map/cond/branch_0_fun/all_to_all | solution.py:390
  55.5 0.0 copy-done.8
  55.5 0.0 copy-done.12
  55.5 0.0 copy-done.16
  55.5 5.9 %ladder_slots.2 = f32[2,4,64,1024]{3,2,1,0:T(8,128)} custom-call(s32[8,1024]{1,0:T(8,128)S(1)} %get-tuple-element.80.row_ref, s32[1024,128]{1,0:T(8,128)S(1)} %get-tuple-element.82.col_ref, f32[16,32,128]{2,1,0:T(8,128)S(1)} %all_to_all.40.got_ref, f32[16,112,128]{2,1,0:T(8,128)S(1)} %all_to_all.41.mid_ref, s32[2]{0:T(128)S(1)} %copy-done.8, ...), custom_call_target="tpu_custom_call" | custom-call | tf_op jit(solution)/shard_map/cond/branch_0_fun/ladder_slots/pallas_call | solution.py:391
Async XLA Ops:
  19.9 35.6 %copy-start.8 = (s32[2]{0:T(128)S(1)}, s32[2]{0:T(128)}, u32[]{:S(2)}) copy-start(s32[2]{0:T(128)} %get-tuple-element.86.i_ref) | copy-start | bytes 28 | tf_op jit(solution)/shard_map/cond
  19.9 35.6 %copy-start.12 = (s32[64]{0:T(128)S(1)}, s32[64]{0:T(128)}, u32[]{:S(2)}) copy-start(s32[64]{0:T(128)} %get-tuple-element.87.j_ref) | copy-start | bytes 772 | tf_op jit(solution)/shard_map/cond
  19.9 35.6 %copy-start.16 = (s32[2]{0:T(128)S(1)}, s32[2]{0:T(128)}, u32[]{:S(2)}) copy-start(s32[2]{0:T(128)} %get-tuple-element.88.l_ref) | copy-start | bytes 28 | tf_op jit(solution)/shard_map/cond

commit v2 on v1

--- a/solution.py
+++ b/solution.py
@@ -1,3 +1,5 @@
+import functools
+
 import jax
 import jax.numpy as jnp
 from jax import lax
@@ -9,6 +11,7 @@
 NN = (((1,), (0,)), ((), ()))
 NT = (((1,), (1,)), ((), ()))
 SLOTS = 32
+TIGHT = 24
 RANKS = 16
 CLS, NUM, SLOT, SPOT, LAB, RANK, BRANCH, BITS = range(8)
 
@@ -43,7 +46,7 @@
     return dot(a, b[0], dims) + dot(a, b[1], dims)
 
 
-def table_kernel(irrep_ref, chol_ref, i_ref, l_ref, pos_ref, row_ref, col_ref, out_ref):
+def table_kernel(irrep_ref, chol_ref, i_ref, l_ref, pos_ref, row_ref, col_ref, order_ref, turn_ref, out_ref):
     cls = irrep_ref[...]
     width = cls.shape[1]
     chunks = width // 128
@@ -73,10 +76,10 @@
     good = (largest <= SLOTS) & (fullest <= RANKS)
     for n in range(l_ref.shape[0]):
         good = good & (parity(bits_col & l_ref[n]) == 1)
-    rank = cand[:, 0:1] + jnp.where(parity(bits_col & (i_ref[0] ^ i_ref[1])) == 1, 0, 16)
+    rank = cand[:, 0:1] + jnp.where(parity(bits_col & (i_ref[0] ^ i_ref[1])) == 1, 0, 32)
+    rank = rank + jnp.where(largest <= TIGHT, 0, 16)
     pick = jnp.min(jnp.where(good, rank.astype(F32), 99.0), axis=0, keepdims=True).astype(I32)
-    dense_branch = jnp.where(l_ref[0] != l_ref[1], 2, 3)
-    branch = jnp.where(pick < 16, 0, jnp.where(pick < 32, 1, dense_branch))
+    branch = jnp.where(pick < 64, pick >> 4, jnp.where(l_ref[0] != l_ref[1], 4, 5))
     bits, side = (pick & 15) >> 1, pick & 1
     small = parity(bits & cls) == side
     group = jnp.zeros_like(cls)
@@ -113,6 +116,9 @@
     for k in range(chunks):
         tile = jnp.concatenate([table[:, 128 * k : 128 * k + 128], jnp.zeros((120, 128), F32)], axis=0)
         col_ref[128 * k : 128 * k + 128, :] = jnp.transpose(tile).astype(I32)
+    spots, numbers = places(row_ref)
+    order_ref[...] = dot(spots, numbers, NT).astype(BF16)
+    turn_ref[...] = dot(numbers, spots, NT).astype(BF16)
     panel_slots(row_ref, col_ref, chol_ref, l_ref, pos_ref, out_ref)
 
 
@@ -149,7 +155,7 @@
     return spots, numbers
 
 
-def ladder_kernel(row_ref, col_ref, got_ref, mid_ref, i_ref, j_ref, l_ref, pos_ref, out_ref):
+def ladder_kernel(count, row_ref, col_ref, order_ref, got_ref, mid_ref, i_ref, j_ref, l_ref, pos_ref, out_ref):
     p, q = pos_ref[0], pos_ref[1]
     cls = row_ref[CLS : CLS + 1, :]
     number = row_ref[NUM : NUM + 1, :]
@@ -163,10 +169,10 @@
         for n in range(2)
     ]
     full = split(jnp.concatenate(full + [one(number == iota((128, width), 0))], axis=0))
-    mids = [mid_ref[:, i, 0:64, :].reshape(width, 128) for i in range(2)]
+    rows, lates = receive(mid_ref, 128, 2 * RANKS, count)
+    mids = [rows[:, 64 * i : 64 * i + 64].reshape(width, 128) for i in range(2)]
     core = dot3(full, split(jnp.concatenate(mids, axis=1)))
-    spots, numbers = places(row_ref)
-    order = dot(numbers, spots, NT).astype(BF16)
+    order = order_ref[...]
     own_panel = unpack(got_ref[pl.ds(q, 1)])
     own_slot = own(col_ref, q, SLOT)
     own_rank = own(col_ref, q, RANK)
@@ -193,7 +199,7 @@
                 jnp.concatenate([jnp.where((lane >> 5) == j, tiles[j], 0.0) for j in range(4)], axis=0)
             )
 
-        late = mid_ref[:, i, 64 : 64 + RANKS, :]
+        late = lates[:, RANKS * i : RANKS * (i + 1)]
         total = jnp.where(odd_lane, 0.0, jnp.sum(late, axis=0))
         late = jnp.where(odd_lane, late.reshape(16 * RANKS, 128), 0.0)
         lanes = slice(128 * i, 128 * i + 128)
@@ -217,6 +223,49 @@
         out_ref[n // 4, n % 4] = result[64 * n : 64 * n + 64]
 
 
+def sent_rows(same, own_rows, count):
+    return same + own_rows if count == SLOTS else -(-(same + own_rows) * count // SLOTS // 8) * 8
+
+
+def send(out_ref, same, different, count):
+    rows, late = same.shape[0], different.shape[1]
+    if count == SLOTS:
+        out_ref[:, 0:rows, :] = jnp.broadcast_to(same[None], (16, rows, 128))
+        out_ref[:, rows : rows + late, :] = different
+        return
+    total = out_ref.shape[1]
+    same = jnp.concatenate([same[:, 32 * j : 32 * j + count] for j in range(4)], axis=1)
+    different = jnp.concatenate([different[:, :, 32 * j : 32 * j + count] for j in range(4)], axis=2)
+    rest = rows - total
+    side = [same[total:, 32 * k : 32 * k + 32] for k in range(3)] + [jnp.zeros((total - 3 * rest, 32), F32)]
+    main = jnp.concatenate([same[0:total], jnp.concatenate(side, axis=0)], axis=1)
+    out_ref[...] = jnp.broadcast_to(main[None], out_ref.shape)
+    for k in range(3):
+        start = 3 * rest + late * k
+        out_ref[:, start : start + late, 96:128] = different[:, :, 32 * k : 32 * k + 32]
+
+
+def receive(mid_ref, rows, late, count):
+    if count == SLOTS:
+        return mid_ref[:, 0:rows, :], mid_ref[:, rows : rows + late, :]
+    total = mid_ref.shape[1]
+    rest = rows - total
+
+    def side(start, size):
+        parts = [mid_ref[:, start + size * k : start + size * (k + 1), 96:128] for k in range(3)]
+        return jnp.concatenate(parts, axis=2)
+
+    def widen(x):
+        gap = jnp.zeros((*x.shape[:2], 32 - count), F32)
+        parts = []
+        for j in range(4):
+            parts += [x[:, :, count * j : count * j + count], gap]
+        return jnp.concatenate(parts, axis=2)
+
+    same = jnp.concatenate([mid_ref[:, :, 0:96], side(0, rest)], axis=1)
+    return widen(same), widen(side(3 * rest, late))
+
+
 def half_products(row_ref, col_ref, amp_ref, got_ref, i_ref, j_ref, pos_ref, high_ref, low_ref):
     p, q = pos_ref[0], pos_ref[1]
     cls = row_ref[CLS : CLS + 1, :]
@@ -250,7 +299,9 @@
     return later, xs[0], xs[1]
 
 
-def half_kernel(row_ref, col_ref, amp_ref, got_ref, i_ref, j_ref, l_ref, pos_ref, out_ref, high_ref, low_ref):
+def half_kernel(
+    count, row_ref, col_ref, order_ref, amp_ref, got_ref, i_ref, j_ref, l_ref, pos_ref, out_ref, high_ref, low_ref
+):
     p, q = pos_ref[0], pos_ref[1]
     label = row_ref[LAB : LAB + 1, 0:128]
     own_cls = own(col_ref, q, CLS)
@@ -266,18 +317,19 @@
     ]
     sums = dot3(split(left[0:32]), split(jnp.concatenate(spread, axis=1)))
     seconds = dot2(left[32:48].astype(BF16), split(jnp.concatenate(both, axis=1)))
-    spots, numbers = places(row_ref)
-    order = dot(spots, numbers, NT).astype(BF16)
+    order = order_ref[...]
+    mains, lates = [], []
     for i in range(2):
         rows = jnp.concatenate([sums[:, 128 * n : 128 * n + 128] for n in range(4 * i, 4 * i + 4)], axis=0)
         by_spot = dot2(order, split(rows), NT).reshape(16, RANKS, 128)
-        out_ref[:, i, 64 : 64 + RANKS, :] = by_spot + seconds[None, :, 128 * i : 128 * i + 128]
-        out_ref[:, i, 0:64, :] = jnp.broadcast_to(
-            jnp.concatenate(firsts[4 * i : 4 * i + 4], axis=1)[None], (16, 64, 128)
-        )
-
-
-def half_paired_kernel(row_ref, col_ref, amp_ref, got_ref, i_ref, j_ref, l_ref, pos_ref, out_ref, high_ref, low_ref):
+        lates.append(by_spot + seconds[None, :, 128 * i : 128 * i + 128])
+        mains.append(jnp.concatenate(firsts[4 * i : 4 * i + 4], axis=1))
+    send(out_ref, jnp.concatenate(mains, axis=0), jnp.concatenate(lates, axis=1), count)
+
+
+def half_paired_kernel(
+    count, row_ref, col_ref, order_ref, amp_ref, got_ref, i_ref, j_ref, l_ref, pos_ref, out_ref, high_ref, low_ref
+):
     p, q = pos_ref[0], pos_ref[1]
     label = row_ref[LAB : LAB + 1, 0:128]
     own_cls = own(col_ref, q, CLS)
@@ -287,15 +339,11 @@
     odd = [jnp.where(later[j], parts[4 + j], parts[j]) for j in range(4)]
     even = [jnp.where(later[j], parts[j], parts[4 + j]) for j in range(4)]
     rows = jnp.concatenate([part[:, 64:96] + jnp.where(own_small, part[:, 0:32], 0.0) for part in odd], axis=1)
-    out_ref[:, 0:64, :] = jnp.broadcast_to(rows[None], (16, 64, 128))
     left = left_factor(col_ref, got_ref, q)
     firsts = jnp.concatenate([part[:, 64:96] for part in even], axis=1)
     seconds = jnp.concatenate([part[:, 32:64] for part in odd], axis=1)
     few = jnp.concatenate([firsts, seconds], axis=1)
     few = dot2(left[32:48].astype(BF16), split(jnp.concatenate([few, few], axis=0)))
-    for k in range(2):
-        few_rows = few[None, :, 128 * k : 128 * k + 128]
-        out_ref[:, 64 + RANKS * k : 64 + RANKS * (k + 1), :] = jnp.broadcast_to(few_rows, (16, RANKS, 128))
     pair_cls = jnp.concatenate([own_cls ^ l_ref[0], own_cls ^ l_ref[1]], axis=0)
     spread = []
     for j in range(4):
@@ -303,12 +351,12 @@
         spread.append(jnp.where(label == (pair_cls ^ even_x[j]), jnp.concatenate([both] * 4, axis=1), 0.0))
     sums = dot3(split(left[0:32]), split(jnp.concatenate(spread, axis=1)))
     sums = jnp.concatenate([sums[:, 128 * j : 128 * j + 128] for j in range(4)], axis=0)
-    spots, numbers = places(row_ref)
-    order = dot(spots, numbers, NT).astype(BF16)
-    out_ref[:, 64 + 2 * RANKS : 64 + 3 * RANKS, :] = dot2(order, split(sums), NT).reshape(16, RANKS, 128)
-
-
-def ladder_paired_kernel(row_ref, col_ref, got_ref, mid_ref, i_ref, j_ref, l_ref, pos_ref, out_ref):
+    order = order_ref[...]
+    rows = jnp.concatenate([rows, few[:, 0:128], few[:, 128:256]], axis=0)
+    send(out_ref, rows, dot2(order, split(sums), NT).reshape(16, RANKS, 128), count)
+
+
+def ladder_paired_kernel(count, row_ref, col_ref, order_ref, got_ref, mid_ref, i_ref, j_ref, l_ref, pos_ref, out_ref):
     p, q = pos_ref[0], pos_ref[1]
     cls = row_ref[CLS : CLS + 1, :]
     number = row_ref[NUM : NUM + 1, :]
@@ -321,12 +369,12 @@
         for n in range(2)
     ]
     full = split(jnp.concatenate(full + [one(number == iota((128, width), 0))], axis=0))
-    core = dot3(full, split(mid_ref[:, 0:64, :].reshape(width, 128)))
-    spots, numbers = places(row_ref)
-    order = dot(numbers, spots, NT).astype(BF16)
-    few = [mid_ref[:, 64 + RANKS * k : 64 + RANKS * (k + 1), :] for k in range(3)]
-    small_rows, second_rows = [dot2(order, split(few[k].reshape(16 * RANKS, 128))) for k in range(2)]
-    total = jnp.concatenate([jnp.sum(few[2], axis=0), jnp.zeros((128 - RANKS, 128), F32)], axis=0)
+    rows, sums = receive(mid_ref, 64 + 2 * RANKS, RANKS, count)
+    core = dot3(full, split(rows[:, 0:64].reshape(width, 128)))
+    order = order_ref[...]
+    few = [rows[:, 64 + RANKS * k : 64 + RANKS * (k + 1)].reshape(16 * RANKS, 128) for k in range(2)]
+    small_rows, second_rows = [dot2(order, split(few[k])) for k in range(2)]
+    total = jnp.concatenate([jnp.sum(sums, axis=0), jnp.zeros((128 - RANKS, 128), F32)], axis=0)
     own_panel = unpack(got_ref[pl.ds(q, 1)])
     own_slot = own(col_ref, q, SLOT)
     own_rank = own(col_ref, q, RANK)
@@ -376,26 +424,26 @@
     return jax.ShapeDtypeStruct(dims, dtype)
 
 
-def compact(kernels, middle, row, col, panel, amplitudes, irrep_i, irrep_j, irrep_l, pos):
+def compact(kernels, same, late, count, row, col, order, turn, panel, amplitudes, irrep_i, irrep_j, irrep_l, pos):
     panel = lax.all_to_all(panel, "ja", split_axis=0, concat_axis=0, tiled=True)
     mid = pl.pallas_call(
-        kernels[0],
-        out_shape=shape(16, *middle, 128),
-        in_specs=[VMEM] * 4 + [SMEM] * 4,
+        functools.partial(kernels[0], count),
+        out_shape=shape(16, sent_rows(same, late, count), 128),
+        in_specs=[VMEM] * 5 + [SMEM] * 4,
         out_specs=VMEM,
         scratch_shapes=[pltpu.VMEM((512, 1024), BF16), pltpu.VMEM((512, 1024), BF16)],
         compiler_params=PARAMS,
         name="half_slots",
-    )(row, col, amplitudes, panel, irrep_i, irrep_j, irrep_l, pos)
+    )(row, col, order, amplitudes, panel, irrep_i, irrep_j, irrep_l, pos)
     mid = lax.all_to_all(mid, "aa", split_axis=0, concat_axis=0, tiled=True)
     return pl.pallas_call(
-        kernels[1],
+        functools.partial(kernels[1], count),
         out_shape=shape(*amplitudes.shape),
-        in_specs=[VMEM] * 4 + [SMEM] * 4,
+        in_specs=[VMEM] * 5 + [SMEM] * 4,
         out_specs=VMEM,
         compiler_params=PARAMS,
         name="ladder_slots",
-    )(row, col, panel, mid, irrep_i, irrep_j, irrep_l, pos)
+    )(row, col, turn, panel, mid, irrep_i, irrep_j, irrep_l, pos)
 
 
 def panel_rows(half_ref, other_ref, core, high_ref, low_ref):
@@ -471,11 +519,17 @@
 def local(amplitudes, chol, irrep_i, irrep_j, irrep_v, irrep_l):
     pos = jnp.stack([lax.axis_index("ja"), lax.axis_index("aa")]).astype(I32)
     width = irrep_v.shape[0]
-    row, col, slots = pl.pallas_call(
+    row, col, order, turn, slots = pl.pallas_call(
         table_kernel,
-        out_shape=(shape(8, width, dtype=I32), shape(width, 128, dtype=I32), shape(16, 32, 128)),
+        out_shape=(
+            shape(8, width, dtype=I32),
+            shape(width, 128, dtype=I32),
+            shape(16 * RANKS, 4 * SLOTS, dtype=BF16),
+            shape(4 * SLOTS, 16 * RANKS, dtype=BF16),
+            shape(16, 32, 128),
+        ),
         in_specs=[VMEM, VMEM, SMEM, SMEM, SMEM],
-        out_specs=(VMEM, VMEM, VMEM),
+        out_specs=(VMEM,) * 5,
         compiler_params=PARAMS,
         name="orbital_table",
     )(irrep_v.reshape(1, width), chol, irrep_i, irrep_l, pos)
@@ -497,12 +551,16 @@
         first, second = panels()
         return run(first) + run(second)
 
-    few = (row, col, slots, amplitudes, irrep_i, irrep_j, irrep_l, pos)
+    few = (row, col, order, turn, slots, amplitudes, irrep_i, irrep_j, irrep_l, pos)
+    paired = ((half_paired_kernel, ladder_paired_kernel), 64 + 2 * RANKS, RANKS)
+    general = ((half_kernel, ladder_kernel), 128, 2 * RANKS)
     return lax.switch(
         row[BRANCH, 0],
         [
-            lambda: compact((half_paired_kernel, ladder_paired_kernel), (64 + 3 * RANKS,), *few),
-            lambda: compact((half_kernel, ladder_kernel), (2, 64 + RANKS), *few),
+            lambda: compact(*paired, TIGHT, *few),
+            lambda: compact(*paired, SLOTS, *few),
+            lambda: compact(*general, TIGHT, *few),
+            lambda: compact(*general, SLOTS, *few),
             together,
             apart,
         ],

time: 61.6 us -> 59 us (0.958)
  blocking collectives: 48.4 us -> 44.9 us
  Pallas kernels: 11.7 us -> 12.5 us
    all_to_all x1, blocking collectives: 32.2 us -> 28.7 us  [compact(): mid = lax.all_to_all(mid, 'aa', split_axis=0, concat_axis=0, tiled=True)]
    pallas_call x2, Pallas kernels: 9.29 us -> 10 us  [the longest x1 6.59 us: compact(): pl.pallas_call(functools.partial(kernels[1], count), out_shape=shape(*amp...]
where the time goes in v2:
time: 59 us; the launch traced here: 58.8 us
  blocking collectives  44.9 us (76%)
  Pallas kernels  12.5 us (21%)
  between operations  0.66 us (1%)
    all_to_all x1, blocking collectives, compact(): mid = lax.all_to_all(mid, 'aa', split_axis=0, concat_axis=0, tiled=True)  28.7 us
    all_to_all x1, blocking collectives, compact(): panel = lax.all_to_all(panel, 'ja', split_axis=0, concat_axis=0, tiled=True)  16.2 us
    pallas_call x1, Pallas kernels, compact(): pl.pallas_call(functools.partial(kernels[1], count), out_shape=shape(*amp...  6.59 us
    pallas_call x1, Pallas kernels, compact(): pl.pallas_call(functools.partial(kernels[0], count), out_shape=shape(16,...  3.45 us
    pallas_call x1, Pallas kernels, local(): pl.pallas_call(table_kernel, out_shape=(shape(8, width, dtype=I32), shape...  2.47 us

profile of v2, /device:TPU:32, one launch (start us, length us, event | category | flops | bytes accessed | tf_op | source)
XLA Modules:
  0.0 58.8 jit_solution(6424032051716951320)
XLA Ops:
  0.0 0.1 pad_add_fusion.pos_ref
  0.1 2.5 %orbital_table.1 = (s32[8,1024]{1,0:T(8,128)S(1)}, s32[1024,128]{1,0:T(8,128)S(1)}, bf16[256,128]{1,0:T(8,128)(2,1)S(1)}, bf16[128,256]{1,0:T(8,128)(2,1)S(1)}, f32[16,32,128]{2,1,0:T(8,128)S(1)}) custom-call(s32[1,1024]{1,0:T(1,128)} %bitcast.14, f32[2,64,1024]{2,1,0:T(8,128)} %chol_ref.1, s32[2]{0:T(128)} %i_ref.1, s32[2]{0:T(128)} %l_ref.1, ...), custom_call_target="tpu_custom_call" | custom-call | tf_op jit(solution)/shard_map/orbital_table/pallas_call | solution.py:522
  2.6 0.5 slice.27
  3.7 55.0 %conditional.1 = (f32[2,4,64,1024]{3,2,1,0:T(8,128)}) conditional(s32[]{:T(128)} %bitcast.10, (f32[16,32,128]{2,1,0:T(8,128)S(1)}, s32[8,1024]{1,0:T(8,128)S(1)}, s32[1024,128]{1,0:T(8,128)S(1)}, bf16[256,128]{1,0:T(8,128)(2,1)S(1)}, f32[2,4,64,1024]{3,2,1,0:T(8,128)}, /*index=5*/s32[2]{0:T(128)}, s32[64]{0:T(128)}, ...), branch_computations={%region_0.0_spmd, %region_1.0_spmd, %region_2.0_spmd, %region_3.0_... | conditional | flops 851972 | bytes 102242560 | solution.py:557
  3.7 16.2 %all_to_all.56.got_ref = f32[16,32,128]{2,1,0:T(8,128)S(1)} all-to-all(f32[16,32,128]{2,1,0:T(8,128)S(1)} %get-tuple-element.134), channel_id=1, replica_groups=mesh['ja'=16,'aa'=16] {'ja'}, dimensions={0} | all-to-all | bytes 524288 | tf_op jit(solution)/shard_map/cond/branch_0_fun/all_to_all | solution.py:428
  20.0 0.0 copy-start.8
  20.0 0.0 copy-start.14
  20.0 0.0 copy-start.20
  20.0 3.4 %half_slots.4 = f32[16,88,128]{2,1,0:T(8,128)S(1)} custom-call(s32[8,1024]{1,0:T(8,128)S(1)} %get-tuple-element.89.row_ref, s32[1024,128]{1,0:T(8,128)S(1)} %get-tuple-element.120.col_ref, bf16[256,128]{1,0:T(8,128)(2,1)S(1)} %get-tuple-element.136.order_ref, f32[2,4,64,1024]{3,2,1,0:T(8,128)} %get-tuple-element.137.amp_ref, ...), custom_call_target="tpu_custom_call" | custom-call | tf_op jit(solution)/shard_map/cond/branch_0_fun/half_slots/pallas_call | solution.py:429
  23.4 28.7 %all_to_all.57.mid_ref = f32[16,88,128]{2,1,0:T(8,128)S(1)} all-to-all(f32[16,88,128]{2,1,0:T(8,128)S(1)} %half_slots.4), channel_id=1, replica_groups=mesh['ja'=16,'aa'=16] {'aa'}, dimensions={0} | all-to-all | bytes 1441792 | tf_op jit(solution)/shard_map/cond/branch_0_fun/all_to_all | solution.py:438
  52.1 0.0 copy-done.8
  52.1 0.0 copy-done.14
  52.2 0.0 copy-done.20
  52.2 6.6 %ladder_slots.4 = f32[2,4,64,1024]{3,2,1,0:T(8,128)} custom-call(s32[8,1024]{1,0:T(8,128)S(1)} %get-tuple-element.89.row_ref, s32[1024,128]{1,0:T(8,128)S(1)} %get-tuple-element.120.col_ref, bf16[128,256]{1,0:T(8,128)(2,1)S(1)} %get-tuple-element.132.order_ref, f32[16,32,128]{2,1,0:T(8,128)S(1)} %all_to_all.56.got_ref, ...), custom_call_target="tpu_custom_call" | custom-call | tf_op jit(solution)/shard_map/cond/branch_0_fun/ladder_slots/pallas_call | solution.py:439
Async XLA Ops:
  20.0 32.2 %copy-start.8 = (s32[2]{0:T(128)S(1)}, s32[2]{0:T(128)}, u32[]{:S(2)}) copy-start(s32[2]{0:T(128)} %get-tuple-element.138.i_ref) | copy-start | bytes 28 | tf_op jit(solution)/shard_map/cond
  20.0 32.2 %copy-start.14 = (s32[64]{0:T(128)S(1)}, s32[64]{0:T(128)}, u32[]{:S(2)}) copy-start(s32[64]{0:T(128)} %get-tuple-element.139.j_ref) | copy-start | bytes 772 | tf_op jit(solution)/shard_map/cond
  20.0 32.2 %copy-start.20 = (s32[2]{0:T(128)S(1)}, s32[2]{0:T(128)}, u32[]{:S(2)}) copy-start(s32[2]{0:T(128)} %get-tuple-element.140.l_ref) | copy-start | bytes 28 | tf_op jit(solution)/shard_map/cond
